TPU v7x, 512 devices: a whole 4x4x16 slice. The times are simulated.
512 devices in a mesh: orb: 16 (over z_lo, core), aux: 32 (over x, y, z_hi).
Axes of the slice: x: 4, y: 4, z: 16 (z_hi: 2, z_lo: 8; z = z_hi * 8 + z_lo), core: 2. Of those that a mesh axis runs over, the one named last changes fastest.
Arguments:
- slab: float32 [512, 256, 256], P('aux', 'orb'), may hold values from -0.375 to 0.375
- pair_blocks: int32 [4, 4], replicated, may hold values from 0 to 1, as said below
- occ_density: float32 [2, 256, 256], P(None, 'orb'), may hold values from -0.375 to 0.375
- vir_density: float32 [2, 256, 256], replicated, may hold values from -0.375 to 0.375
Outputs:
- response: float32 [2, 512, 512], P(None, 'aux')
Inputs may be any that keep to these rules, and one draw needn't show every extreme that they name: `pair_blocks`: blocks on the diagonal are always kept.
All inputs are finite; a program needn't handle non-finite values.
Results may differ from a plain program's by a relative error of at most 0.0001.
Values sent between devices are 32-bit elements; how exact they have to be, the bound alone decides.
No kernel may reach another device: no remote copies, remote signals or barrier semaphores. Data moves between devices by JAX's collectives and lax.ppermute only.
A program may use at most 64 MiB of HBM per device.

v0:
```python
import jax
import jax.numpy as jnp
from jax import lax
from jax.sharding import PartitionSpec as P


def body(slab, pair_blocks, occ_density, vir_density):
    highest = lax.Precision.HIGHEST
    norbit = vir_density.shape[1]
    own_rows = slab.shape[1]
    count = pair_blocks.shape[0]
    width = norbit // count
    expanded = jnp.broadcast_to(
        pair_blocks.astype(jnp.float32)[:, None, :, None], (count, width, count, width)
    ).reshape(norbit, norbit)
    row_mask = lax.dynamic_slice_in_dim(expanded, lax.axis_index("orb") * own_rows, own_rows, 0)
    masked = slab * row_mask[None]
    mixed_part = jnp.einsum(
        "pmn,tnb->tpmb",
        lax.all_gather(masked, "orb", axis=1, tiled=True),
        vir_density,
        precision=highest,
    )
    paired = jnp.einsum("tam,tpmb->tpab", occ_density, mixed_part, precision=highest)
    moved = lax.all_to_all(paired, "aux", split_axis=3, concat_axis=1, tiled=True)
    slab_moved = lax.all_to_all(masked, "aux", split_axis=2, concat_axis=0, tiled=True)
    flat_pairs = moved.reshape(moved.shape[0], moved.shape[1], moved.shape[2] * moved.shape[3])
    flat_slab = slab_moved.reshape(slab_moved.shape[0], slab_moved.shape[1] * slab_moved.shape[2])
    partial_sum = jnp.einsum("tpk,qk->tpq", flat_pairs, flat_slab, precision=highest)
    rows_here = lax.psum_scatter(partial_sum, "aux", scatter_dimension=1, tiled=True)
    return lax.psum(rows_here, "orb")


def solution(mesh):
    in_specs = (P("aux", "orb", None), P(), P(None, "orb", None), P())
    out_specs = P(None, "aux", None)
    return jax.shard_map(body, mesh=mesh, in_specs=in_specs, out_specs=out_specs, check_vma=False)
```

profile of v0, /device:TPU:1, one launch (start us, length us, event | category | flops | bytes accessed | tf_op | source)
XLA Modules:
  0.0 775.2 jit_solution(174256216242354413)
XLA Ops:
  6.5 0.0 copy-start
  6.5 0.0 all-gather.2.cloned.1.call-start
  6.5 0.7 convert_element_type.3
  7.3 0.1 broadcast_in_dim.2
  7.4 0.3 reshape.13
  7.8 1.7 broadcast_multiply_fusion
  9.5 0.0 all-gather.2.cloned.1.call-update
  9.5 2.2 copy.16
  11.7 1.5 reshape.22
  13.2 21.3 %all-to-all-start.1 = ((f32[32,1,2048]{2,1,0:T(1,128)}), f32[32,1,2048]{2,1,0:T(1,128)S(1)}, u32[]{:S(2)}, u32[]{:S(2)}) async-start(f32[32,1,2048]{2,1,0:T(1,128)} %reshape.22), calls=%async_computation.1 | async-start | bytes 524288 | tf_op jit(solution)/shard_map/all_to_all | solution.py:26
  34.5 0.0 copy-start.1
  34.5 88.8 %all-gather.2.cloned.1.call-done = f32[16,256,256]{2,1,0:T(8,128)} async-done(((f32[16,16,256]{2,1,0:T(8,128)}), f32[16,256,256]{2,1,0:T(8,128)}) %all-gather.2.cloned.1.call-update) | async-done | bytes 4194320 | tf_op jit(solution)/shard_map/all_gather | solution.py:20
  123.3 0.0 copy-done
  123.3 9.1 %fusion.2 = f32[16,256,2,256]{3,1,0,2:T(8,128)S(1)} fusion(f32[16,256,256]{2,1,0:T(8,128)} %all-gather.2.cloned.1.call-done, f32[2,256,256]{2,1,0:T(8,128)S(1)} %copy-done), kind=kOutput, calls=%fused_computation.2 | convolution fusion | flops 6442450944 | bytes 13107200 | tf_op jit(solution)/shard_map/pmn,tnb->tpmb/dot_general | solution.py:18
  132.4 0.0 copy-done.1
  132.4 4.5 fusion.4
  136.9 4.4 copy.13
  141.2 4.2 reshape.20
  145.4 0.0 all-to-all-done.1
  145.4 15.2 %all-to-all-start = ((f32[32,1,4096]{2,1,0:T(1,128)}), f32[32,1,4096]{2,1,0:T(1,128)S(1)}, u32[]{:S(2)}, u32[]{:S(2)}) async-start(f32[32,1,4096]{2,1,0:T(1,128)} %reshape.20), calls=%async_computation | async-start | bytes 1048576 | tf_op jit(solution)/shard_map/all_to_all | solution.py:25
  160.6 0.3 reduce-scatter.2.cloned.1.call-start
  160.9 0.5 broadcast.2
  161.4 1.3 reduce.1
  162.7 0.7 reshape.23
  163.4 2.6 copy.18
  166.0 3.1 reshape.15
  169.1 10.1 %all-to-all-done = f32[32,1,4096]{2,1,0:T(1,128)S(1)} async-done(((f32[32,1,4096]{2,1,0:T(1,128)}), f32[32,1,4096]{2,1,0:T(1,128)S(1)}, u32[]{:S(2)}, u32[]{:S(2)}) %all-to-all-start) | async-done | bytes 524320 | tf_op jit(solution)/shard_map/all_to_all | solution.py:25
  179.2 1.9 reduce
  181.1 2.8 reshape.21
  183.8 6.4 copy.15
  190.2 4.5 reshape.14
  194.7 3.2 fusion.8
  197.9 0.0 reduce-scatter.2.cloned.1.call-update
  197.9 0.0 all-reduce.2.cloned.1.call-start
  198.0 336.5 %reduce-scatter.2.cloned.1.call-done = f32[2,16,512]{2,1,0:T(8,128)} async-done(((f32[2,512,512]{2,1,0:T(8,128)}), f32[2,16,512]{2,1,0:T(8,128)}) %reduce-scatter.2.cloned.1.call-update) | async-done | bytes 65552 | tf_op jit(solution)/shard_map/reduce_scatter | solution.py:30
  534.5 0.0 all-reduce.2.cloned.1.call-update
  534.5 232.7 %all-reduce.2.cloned.1.call-done = f32[2,16,512]{2,1,0:T(8,128)} async-done(((f32[2,16,512]{2,1,0:T(8,128)}), f32[2,16,512]{2,1,0:T(8,128)}) %all-reduce.2.cloned.1.call-update) | async-done | bytes 65552 | tf_op jit(solution)/shard_map/psum | solution.py:31
  767.1 1.5 copy.29
  (1 shorter events, 0.0 us)
Async XLA Ops:
  6.5 116.7 %copy-start = (f32[2,256,256]{2,1,0:T(8,128)S(1)}, f32[2,256,256]{2,1,0:T(8,128)}, u32[]{:S(2)}) copy-start(f32[2,256,256]{2,1,0:T(8,128)} %param.7) | copy-start | bytes 1572868
  6.5 116.7 %all-gather.2.cloned.1.call-start = ((), (), s32[]{:S(2)}) async-start(), calls=%async_computation.3 | async-start | bytes 4456448 | tf_op jit(solution)/shard_map/all_gather | solution.py:20
  13.2 132.3 %all-to-all-start.1 = ((f32[32,1,2048]{2,1,0:T(1,128)}), f32[32,1,2048]{2,1,0:T(1,128)S(1)}, u32[]{:S(2)}, u32[]{:S(2)}) async-start(f32[32,1,2048]{2,1,0:T(1,128)} %reshape.22), calls=%async_computation.1 | async-start | bytes 524288 | tf_op jit(solution)/shard_map/all_to_all | solution.py:26
  34.5 97.9 %copy-start.1 = (f32[2,16,256]{2,1,0:T(8,128)S(1)}, f32[2,16,256]{2,1,0:T(8,128)}, u32[]{:S(2)}) copy-start(f32[2,16,256]{2,1,0:T(8,128)} %param.6) | copy-start | bytes 98308
  145.4 33.7 %all-to-all-start = ((f32[32,1,4096]{2,1,0:T(1,128)}), f32[32,1,4096]{2,1,0:T(1,128)S(1)}, u32[]{:S(2)}, u32[]{:S(2)}) async-start(f32[32,1,4096]{2,1,0:T(1,128)} %reshape.20), calls=%async_computation | async-start | bytes 1048576 | tf_op jit(solution)/shard_map/all_to_all | solution.py:25
  160.6 373.9 %reduce-scatter.2.cloned.1.call-start = ((), (), s32[]{:S(2)}) async-start(), calls=%async_computation.4 | async-start | bytes 2162688 | tf_op jit(solution)/shard_map/reduce_scatter | solution.py:30
  197.9 569.2 %all-reduce.2.cloned.1.call-start = ((), (), s32[]{:S(2)}) async-start(), calls=%async_computation.5 | async-start | bytes 131072 | tf_op jit(solution)/shard_map/psum | solution.py:31
Sparse Core Ops, SparseCore 0:
  9.6 113.6 all-gather.1
  198.1 336.3 reduce-scatter.1
  537.6 229.4 all-reduce.1
where the time goes:
time: 776 us; the launch traced here: 775 us
  waiting for transfers between devices  668 us (86%)
  starting transfers between devices  36.8 us (5%)
  local copies, waits for them, and re-layouts  34.8 us (4%)
  matrix products  16.8 us (2%)
  between operations  13.2 us (2%)
    reduce_scatter x1, waiting for transfers between devices, body(): lax.psum_scatter(partial_sum, 'aux', scatter_dimension=1, tiled=True)  336 us
    psum x1, waiting for transfers between devices, body(): return lax.psum(rows_here, 'orb')  233 us
    all_gather x1, waiting for transfers between devices, body(): lax.all_gather(masked, 'orb', axis=1, tiled=True)  88.8 us
    all_to_all x1, starting transfers between devices, body(): lax.all_to_all(masked, 'aux', split_axis=2, concat_axis=0, tiled=True)  21.3 us
  transfers between devices with their start and end apart: 5, of which 4 were waited for; matrix products, arithmetic and copies ran while one was open for 4% of the time, Pallas kernels for 0%

commit v1 on v0

v1 whole, which is shorter than its diff:
```python
import jax
import jax.numpy as jnp
from jax import lax
from jax.experimental import pallas as pl
from jax.experimental.pallas import tpu as pltpu
from jax.sharding import Mesh, PartitionSpec as P

NT_DIMS = (((1,), (1,)), ((), ()))
NN_DIMS = (((1,), (0,)), ((), ()))


def split(value):
    high = value.astype(jnp.bfloat16)
    return high, (value - high.astype(jnp.float32)).astype(jnp.bfloat16)


def dot3(left, right, dims):
    left_high, left_low = split(left)
    right_high, right_low = split(right)

    def dot(a, b):
        return lax.dot_general(a, b, dims, preferred_element_type=jnp.float32)

    return dot(left_high, right_high) + (dot(left_low, right_high) + dot(left_high, right_low))


def pairing(times, slab_ref, vir_ref, occ_ref, out_ref):
    peers, _, rows, width = out_ref.shape
    slab = slab_ref[...].reshape(vir_ref.shape[1:])
    for t in range(times):
        mixed = dot3(slab, vir_ref[t], NN_DIMS)
        paired = dot3(occ_ref[t], mixed, NN_DIMS)
        out_ref[:, t] = paired.reshape(peers, rows, width)


def respond(paired_ref, slab_ref, out_ref):
    step = pl.program_id(0)
    sources, times = paired_ref.shape[:2]
    halves, _, count, width = slab_ref.shape
    run = count // 16
    right = slab_ref[...].reshape(halves, 16, run, width)
    right = jnp.swapaxes(right, 0, 1).reshape(halves * count, width)
    left = jnp.concatenate([paired_ref[:, t, pl.ds(step, 1), :].reshape(sources, width) for t in range(times)], axis=0)
    total = dot3(left, right, NT_DIMS)
    lanes = out_ref.shape[2]

    @pl.when(step == 0)
    def _():
        out_ref[...] = jnp.zeros_like(out_ref)

    pieces = total.shape[1] // lanes
    for t in range(times):
        for k in range(pieces):
            out_ref[:, t * pieces + k, :] += total[t * sources:(t + 1) * sources, k * lanes:(k + 1) * lanes]


def body(slab, pair_blocks, occ_density, vir_density):
    aux_here, rows_here, norbit = slab.shape
    times = occ_density.shape[0]
    near, cores, planes, halves = 8, 2, 16, 2
    count = pair_blocks.shape[0]
    width = norbit // count
    block = lax.axis_index(("zl", "c")) * rows_here // width
    row_mask = jnp.repeat(lax.dynamic_index_in_dim(pair_blocks, block, 0, keepdims=False).astype(jnp.float32), width)
    masked = slab * row_mask[None, None, :]

    by_row = lax.all_to_all(jnp.swapaxes(masked, 0, 1), ("x", "y"), 0, 0, tiled=True)
    by_row = by_row.reshape(planes * aux_here, norbit)
    gathered = lax.all_gather(by_row, ("zh", "zl"), axis=0, tiled=True)
    gathered = gathered.reshape(halves, near, planes * aux_here, norbit)

    occ_all = lax.all_gather(occ_density, ("zl", "c"), axis=0, tiled=False)
    occ_all = occ_all.reshape(near, cores, times, rows_here, norbit).transpose(2, 1, 3, 0, 4).reshape(times, norbit, norbit)
    own = lax.all_to_all(masked, ("zl", "c"), 0, 0, tiled=True)
    vmem = pl.BlockSpec(memory_space=pltpu.VMEM)
    paired = pl.pallas_call(
        lambda *refs: pairing(times, *refs),
        out_shape=jax.ShapeDtypeStruct((cores * planes, times, near, norbit), jnp.float32),
        in_specs=[vmem, vmem, vmem],
        out_specs=vmem,
        compiler_params=pltpu.CompilerParams(vmem_limit_bytes=32 << 20),
        cost_estimate=pl.CostEstimate(flops=12 * times * norbit**3, bytes_accessed=2 << 20, transcendentals=0),
    )(own, vir_density, occ_all)
    paired = lax.all_to_all(paired.reshape(cores * planes, times * near, norbit), ("c", "x", "y"), 0, 0, tiled=True)
    paired = paired.reshape(cores * planes, times, near, norbit)

    total_aux = halves * planes * aux_here
    lanes = 128
    partial = pl.pallas_call(
        respond,
        grid=(near,),
        out_shape=jax.ShapeDtypeStruct((cores * planes, times * total_aux // lanes, lanes), jnp.float32),
        in_specs=[
            pl.BlockSpec((cores * planes, times, near, norbit), lambda s: (0, 0, 0, 0)),
            pl.BlockSpec((halves, 1, planes * aux_here, norbit), lambda s: (0, s, 0, 0)),
        ],
        out_specs=pl.BlockSpec((cores * planes, times * total_aux // lanes, lanes), lambda s: (0, 0, 0)),
        compiler_params=pltpu.CompilerParams(vmem_limit_bytes=32 << 20),
        cost_estimate=pl.CostEstimate(flops=1 << 28, bytes_accessed=5 << 20, transcendentals=0),
    )(paired, gathered)
    rows = jnp.sum(lax.all_to_all(partial, ("c", "x", "y"), 0, 0, tiled=True), axis=0)
    spread = jnp.broadcast_to(rows[None], (near * cores,) + rows.shape)
    everyone = lax.all_to_all(spread, ("zl", "c"), 0, 0, tiled=True)
    return jnp.swapaxes(everyone.reshape(aux_here, times, total_aux), 0, 1)


def solution(mesh):
    fine = Mesh(mesh.devices.reshape(8, 2, 4, 4, 2), ("zl", "c", "x", "y", "zh"))
    orb, aux = ("zl", "c"), ("x", "y", "zh")
    in_specs = (P(aux, orb, None), P(), P(None, orb, None), P())
    out_specs = P(None, aux, None)
    return jax.shard_map(body, mesh=fine, in_specs=in_specs, out_specs=out_specs, check_vma=False)
```

time: 776 us -> 158 us (0.20)
  waiting for transfers between devices: 668 us -> 13.9 us
  blocking collectives: 0 us -> 103 us
  local copies, waits for them, and re-layouts: 34.8 us -> 3.5 us
  starting transfers between devices: 36.8 us -> 14.7 us
  matrix products: 16.8 us -> 0 us
    reduce_scatter x1 -> x0, waiting for transfers between devices: 336 us -> none  [body(): lax.psum_scatter(partial_sum, 'aux', scatter_dimension=1, tiled=True)]
    psum x1 -> x0, waiting for transfers between devices: 233 us -> none  [body(): return lax.psum(rows_here, 'orb')]
    all_gather x1, waiting for transfers between devices: 88.8 us -> 13.9 us  [body(): gathered = lax.all_gather(by_row, ('zh', 'zl'), axis=0, tiled=True)]
    all_to_all x0 -> x4, blocking collectives: none -> 64 us  [the longest x1 18.1 us: body(): lax.all_to_all(partial, ('c', 'x', 'y'), 0, 0, tiled=True)]
    all_gather x0 -> x1, blocking collectives: none -> 39 us  [body(): occ_all = lax.all_gather(occ_density, ('zl', 'c'), axis=0, tiled=False)]
    all_to_all x2 -> x1, starting transfers between devices: 36.5 us -> 14.7 us  [body(): own = lax.all_to_all(masked, ('zl', 'c'), 0, 0, tiled=True)]
    dot_general x3 -> x0, matrix products: 16.8 us -> none  [the longest x1 9.12 us: body(): jnp.einsum('pmn,tnb->tpmb', lax.all_gather(masked, 'orb', axis=1, tiled=T...]
    all_to_all x2 -> x1, waiting for transfers between devices: 10.1 us -> 0.01 us  [body(): own = lax.all_to_all(masked, ('zl', 'c'), 0, 0, tiled=True)]
  transfers between devices with their start and end apart: 5 -> 2, of which waited for: 4 -> 1; matrix products, arithmetic and copies ran while one was open for 4% -> 1% of each run, Pallas kernels for 0% -> 1%
where the time goes in v1:
time: 158 us; the launch traced here: 157 us
  blocking collectives  103 us (65%)
  starting transfers between devices  14.7 us (9%)
  waiting for transfers between devices  13.9 us (9%)
  between operations  13.4 us (8%)
  Pallas kernels  5.28 us (3%)
  local copies, waits for them, and re-layouts  3.5 us (2%)
  other arithmetic  3.45 us (2%)
    all_gather x1, blocking collectives, body(): occ_all = lax.all_gather(occ_density, ('zl', 'c'), axis=0, tiled=False)  39 us
    all_to_all x1, blocking collectives, body(): lax.all_to_all(partial, ('c', 'x', 'y'), 0, 0, tiled=True)  18.1 us
    all_to_all x1, blocking collectives, body(): everyone = lax.all_to_all(spread, ('zl', 'c'), 0, 0, tiled=True)  16.9 us
    all_to_all x1, blocking collectives, body(): lax.all_to_all(jnp.swapaxes(masked, 0, 1), ('x', 'y'), 0, 0, tiled=True)  14.8 us
    all_to_all x1, starting transfers between devices, body(): own = lax.all_to_all(masked, ('zl', 'c'), 0, 0, tiled=True)  14.7 us
    all_to_all x1, blocking collectives, body(): lax.all_to_all(paired.reshape(cores * planes, times * near, norbit), ('c'...  14.2 us
    all_gather x1, waiting for transfers between devices, body(): gathered = lax.all_gather(by_row, ('zh', 'zl'), axis=0, tiled=True)  13.9 us
    pallas_call x1, Pallas kernels, body(): pl.pallas_call(respond, grid=(near,), out_shape=jax.ShapeDtypeStruct((cor...  4.4 us
  transfers between devices with their start and end apart: 2, of which 1 were waited for; matrix products, arithmetic and copies ran while one was open for 1% of the time, Pallas kernels for 1%

profile of v1, /device:TPU:1, one launch (start us, length us, event | category | flops | bytes accessed | tf_op | source)
XLA Modules:
  0.0 157.3 jit_solution(14423495532309214458)
XLA Ops:
  6.5 0.0 copy-start.1
  6.5 0.0 all-gather.3.cloned.1.call-start
  6.5 0.7 convert_bitcast_fusion
  7.3 0.1 broadcast_in_dim.4
  7.4 0.1 mul.18
  7.4 1.0 fusion
  8.4 0.2 copy.10
  8.6 14.8 %all_to_all.25 = f32[16,16,256]{2,1,0:T(8,128)} all-to-all(f32[16,16,256]{2,1,0:T(8,128)S(1)} %copy.10), channel_id=1, replica_groups=mesh['zl'=8,'c'=2,'x'=4,'y'=4,'zh'=2] {'x','y'}, dimensions={0} | all-to-all | bytes 524288 | tf_op jit(solution)/shard_map/all_to_all | solution.py:67
  23.4 0.0 all-gather.3.cloned.1.call-update
  23.4 1.7 %broadcast_multiply_fusion = f32[16,16,256]{2,1,0:T(8,128)} fusion(f32[16,16,256]{2,1,0:T(8,128)} %param.4, f32[256]{0:T(256)S(1)} %mul.18), kind=kLoop, calls=%fused_computation | loop fusion | flops 65536 | bytes 525312 | tf_op jit(solution)/shard_map/mul | solution.py:65
  25.1 14.7 %all-to-all-start = ((f32[16,16,256]{2,1,0:T(8,128)}), f32[16,16,256]{2,1,0:T(8,128)S(1)}, u32[]{:S(2)}, u32[]{:S(2)}) async-start(f32[16,16,256]{2,1,0:T(8,128)} %broadcast_multiply_fusion), calls=%async_computation | async-start | bytes 524288 | tf_op jit(solution)/shard_map/all_to_all | solution.py:74
  39.8 39.0 %all-gather = f32[32,16,256]{2,1,0:T(8,128)S(1)} all-gather(f32[2,16,256]{2,1,0:T(8,128)} %param.6), channel_id=2, replica_groups=mesh['zl'=8,'c'=2,'x'=4,'y'=4,'zh'=2] {'zl','c'}, dimensions={0}, use_global_device_ids=true | all-gather | bytes 557056 | tf_op jit(solution)/shard_map/all_gather | solution.py:72
  78.8 0.3 copy.9
  79.2 0.0 all-to-all-done.refs_0_
  79.2 0.0 copy-done.1
  79.2 0.9 shard_map.46
  80.1 14.2 %all_to_all.26 = f32[32,16,256]{2,1,0:T(8,128)S(1)} all-to-all(f32[32,16,256]{2,1,0:T(8,128)S(1)} %bitcast.16), channel_id=1, replica_groups=mesh['zl'=8,'c'=2,'x'=4,'y'=4,'zh'=2] {'c','x','y'}, dimensions={0} | all-to-all | bytes 1048576 | tf_op jit(solution)/shard_map/all_to_all | solution.py:84
  94.2 13.9 %all-gather.3.cloned.1.call-done = f32[4096,256]{1,0:T(8,128)} async-done(((f32[256,256]{1,0:T(8,128)}), f32[4096,256]{1,0:T(8,128)}) %all-gather.3.cloned.1.call-update) | async-done | bytes 4194320 | tf_op jit(solution)/shard_map/all_gather | solution.py:69
  108.2 0.0 copy-start
  108.2 2.2 %copy-done = f32[4096,256]{1,0:T(8,128)S(1)} copy-done((f32[4096,256]{1,0:T(8,128)S(1)}, f32[4096,256]{1,0:T(8,128)}, u32[]{:S(2)}) %copy-start) | copy-done | bytes 4194328
  110.3 4.4 %shard_map.47 = f32[32,8,128]{2,1,0:T(8,128)S(1)} custom-call(f32[32,2,8,256]{3,2,1,0:T(8,128)S(1)} %bitcast.15, f32[2,8,256,256]{3,2,1,0:T(8,128)S(1)} %bitcast.13), custom_call_target="tpu_custom_call" | custom-call | flops 268435456 | bytes 5242880 | tf_op jit(solution)/shard_map/pallas_call | solution.py:89
  114.8 18.1 %all_to_all.27 = f32[32,8,128]{2,1,0:T(8,128)S(1)} all-to-all(f32[32,8,128]{2,1,0:T(8,128)S(1)} %shard_map.47), channel_id=1, replica_groups=mesh['zl'=8,'c'=2,'x'=4,'y'=4,'zh'=2] {'c','x','y'}, dimensions={0} | all-to-all | bytes 262144 | tf_op jit(solution)/shard_map/all_to_all | solution.py:101
  132.9 16.9 %all_to_all.28 = f32[16,8,128]{2,1,0:T(8,128)S(1)} all-to-all(f32[16,8,128]{2,1,0:T(8,128)S(1)} %broadcast_in_dim.10), channel_id=1, replica_groups=mesh['zl'=8,'c'=2,'x'=4,'y'=4,'zh'=2] {'zl','c'}, dimensions={0} | all-to-all | bytes 131072 | tf_op jit(solution)/shard_map/all_to_all | solution.py:103
  149.8 0.6 copy.11
  (3 shorter events, 0.1 us)
Async XLA Ops:
  6.5 72.6 %copy-start.1 = (f32[2,256,256]{2,1,0:T(8,128)S(1)}, f32[2,256,256]{2,1,0:T(8,128)}, u32[]{:S(2)}) copy-start(f32[2,256,256]{2,1,0:T(8,128)} %refs_1_.1) | copy-start | bytes 1572868
  6.5 101.6 %all-gather.3.cloned.1.call-start = ((), (), s32[]{:S(2)}) async-start(), calls=%async_computation.5 | async-start | bytes 4456448 | tf_op jit(solution)/shard_map/all_gather | solution.py:69
  25.1 54.0 %all-to-all-start = ((f32[16,16,256]{2,1,0:T(8,128)}), f32[16,16,256]{2,1,0:T(8,128)S(1)}, u32[]{:S(2)}, u32[]{:S(2)}) async-start(f32[16,16,256]{2,1,0:T(8,128)} %broadcast_multiply_fusion), calls=%async_computation | async-start | bytes 524288 | tf_op jit(solution)/shard_map/all_to_all | solution.py:74
  108.2 2.2 %copy-start = (f32[4096,256]{1,0:T(8,128)S(1)}, f32[4096,256]{1,0:T(8,128)}, u32[]{:S(2)}) copy-start(f32[4096,256]{1,0:T(8,128)} %all-gather.3.cloned.1.call-done) | copy-start | bytes 12582916
Sparse Core Ops, SparseCore 0:
  23.6 84.5 all-gather.2

commit v2 on v0

v2 whole, which is shorter than its diff:
```python
import jax
import jax.numpy as jnp
from jax import lax
from jax.experimental import pallas as pl
from jax.experimental.pallas import tpu as pltpu
from jax.sharding import Mesh, PartitionSpec as P

NT_DIMS = (((1,), (1,)), ((), ()))
NN_DIMS = (((1,), (0,)), ((), ()))
LANES = 128
VMEM = pl.BlockSpec(memory_space=pltpu.VMEM)
SMEM = pl.BlockSpec(memory_space=pltpu.SMEM)
PARAMS = pltpu.CompilerParams(vmem_limit_bytes=32 << 20)
WIDE = pltpu.CompilerParams(vmem_limit_bytes=60 << 20)


def split(value):
    high = value.astype(jnp.bfloat16)
    return high, (value - high.astype(jnp.float32)).astype(jnp.bfloat16)


def dot3(left, right, dims):
    def dot(a, b):
        return lax.dot_general(a, b, dims, preferred_element_type=jnp.float32)

    return dot(left[0], right[0]) + (dot(left[1], right[0]) + dot(left[0], right[1]))


def block_row(blocks_ref, block, norbit):
    count = blocks_ref.shape[1]
    lane = lax.broadcasted_iota(jnp.int32, (1, norbit), 1) // (norbit // count)
    mask = jnp.zeros((1, norbit), jnp.float32)
    for k in range(count):
        mask = jnp.where(lane == k, blocks_ref[block, k].astype(jnp.float32), mask)
    return mask


def by_rows(blocks_ref, slab_ref, rows_ref):
    _, own_rows, norbit = slab_ref.shape
    place = (lax.axis_index("g") * 2 + lax.axis_index("b")) * 2 + lax.axis_index("c")
    mask = block_row(blocks_ref, lax.div(place * own_rows, norbit // blocks_ref.shape[0]), norbit)
    for m in range(own_rows):
        rows_ref[m] = slab_ref[:, m, :] * mask


def pairing(blocks_ref, slab_ref, occ_ref, vir_ref, out_ref):
    peers, times, rows, norbit = occ_ref.shape
    count = blocks_ref.shape[0]
    mask = jnp.concatenate(
        [jnp.broadcast_to(block_row(blocks_ref, j, norbit), (norbit // count, norbit)) for j in range(count)], axis=0
    )
    slab = split(slab_ref[...].reshape(norbit, norbit) * mask)
    dests = out_ref.shape[0]
    bands = norbit // dests
    for t in range(times):
        mixed = split(dot3(slab, split(vir_ref[t]), NN_DIMS))
        paired = dot3(split(occ_ref[:, t].reshape(norbit, norbit)), mixed, NN_DIMS)
        for g in range(bands):
            out_ref[:, t * bands + g, :] = paired[g * dests:(g + 1) * dests]


def respond(paired_ref, slab_ref, out_ref, total):
    step = pl.program_id(0)
    sources, planes = paired_ref.shape[0], 16
    halves, _, count, norbit = slab_ref.shape
    bands = pl.num_programs(0)
    run = count // planes

    @pl.when(step == 0)
    def _():
        total[...] = jnp.zeros_like(total)

    rows = [paired_ref[:, pl.ds(i * bands + step, 1), :].reshape(sources, norbit) for i in range(2)]
    right = jnp.swapaxes(slab_ref[...].reshape(halves, planes, run, norbit), 0, 1).reshape(halves * count, norbit)
    total[...] += dot3(split(jnp.concatenate(rows, axis=0)), split(right), NT_DIMS)

    @pl.when(step == bands - 1)
    def _():
        whole = total[...].reshape(2, sources, halves * count)
        chunks = whole.shape[-1] // LANES
        for i in range(2):
            for k in range(chunks):
                out_ref[:, i * chunks + k, :] = whole[i, :, k * LANES:(k + 1) * LANES]


def body(slab, pair_blocks, occ_density, vir_density):
    aux_here, own_rows, norbit = slab.shape
    times = occ_density.shape[0]
    bands, pairs, cores, planes, halves = 4, 2, 2, 16, 2
    dests = pairs * cores * planes
    orb, share, f32 = ("g", "b", "c"), ("b", "c", "x", "y"), jnp.float32

    by_row = pl.pallas_call(
        by_rows,
        out_shape=jax.ShapeDtypeStruct((own_rows, aux_here, norbit), f32),
        in_specs=[SMEM, VMEM],
        out_specs=VMEM,
        compiler_params=WIDE,
    )(pair_blocks, slab)
    own = lax.all_to_all(by_row, ("x", "y"), 0, 0, tiled=True).reshape(planes * aux_here, norbit)
    gathered = lax.all_gather(own, ("zh", "g"), axis=0, tiled=True).reshape(halves, bands, planes * aux_here, norbit)

    later, later_occ, own = lax.optimization_barrier((slab, occ_density, own))
    first = lax.all_to_all(later, orb, 0, 0, tiled=True)
    occ_all = lax.all_gather(later_occ, orb, axis=0, tiled=False)
    paired = pl.pallas_call(
        pairing,
        out_shape=jax.ShapeDtypeStruct((dests, 2 * bands, norbit), f32),
        in_specs=[SMEM, VMEM, VMEM, VMEM],
        out_specs=VMEM,
        compiler_params=PARAMS,
    )(pair_blocks, first, occ_all, vir_density)
    paired = lax.all_to_all(paired, share, 0, 0, tiled=True)

    total_aux = halves * planes * aux_here
    per_row = times * total_aux // LANES
    partial = pl.pallas_call(
        respond,
        grid=(bands,),
        out_shape=jax.ShapeDtypeStruct((dests, per_row, LANES), f32),
        in_specs=[
            pl.BlockSpec((dests, 2 * bands, norbit), lambda s: (0, 0, 0)),
            pl.BlockSpec((halves, 1, planes * aux_here, norbit), lambda s: (0, s, 0, 0)),
        ],
        out_specs=pl.BlockSpec((dests, per_row, LANES), lambda s: (0, 0, 0)),
        scratch_shapes=[pltpu.VMEM((2 * dests, total_aux), f32)],
        compiler_params=PARAMS,
    )(paired.reshape(dests, 2 * bands, norbit), gathered)
    summed = lax.all_to_all(partial, share, 0, 0, tiled=True)
    row = jnp.sum(summed, axis=0)
    spread = jnp.broadcast_to(row[None], (aux_here,) + row.shape)
    everyone = lax.all_to_all(spread, orb, 0, 0, tiled=True)
    return jnp.swapaxes(everyone.reshape(aux_here, times, total_aux), 0, 1)


def solution(mesh):
    fine = Mesh(mesh.devices.reshape(4, 2, 2, 4, 4, 2), ("g", "b", "c", "x", "y", "zh"))
    orb, aux = ("g", "b", "c"), ("x", "y", "zh")
    in_specs = (P(aux, orb, None), P(), P(None, orb, None), P())
    out_specs = P(None, aux, None)
    return jax.shard_map(body, mesh=fine, in_specs=in_specs, out_specs=out_specs, check_vma=False)
```

time: 776 us -> 147 us (0.19)
  waiting for transfers between devices: 668 us -> 0.02 us
  blocking collectives: 0 us -> 111 us
  local copies, waits for them, and re-layouts: 34.8 us -> 2.29 us
  starting transfers between devices: 36.8 us -> 14.7 us
  matrix products: 16.8 us -> 0 us
    reduce_scatter x1 -> x0, waiting for transfers between devices: 336 us -> none  [body(): lax.psum_scatter(partial_sum, 'aux', scatter_dimension=1, tiled=True)]
    psum x1 -> x0, waiting for transfers between devices: 233 us -> none  [body(): return lax.psum(rows_here, 'orb')]
    all_gather x1, waiting for transfers between devices: 88.8 us -> 0.01 us  [body(): lax.all_gather(own, ('zh', 'g'), axis=0, tiled=True)]
    all_to_all x0 -> x4, blocking collectives: none -> 66.3 us  [the longest x1 20.9 us: body(): paired = lax.all_to_all(paired, share, 0, 0, tiled=True)]
    all_gather x0 -> x1, blocking collectives: none -> 44.3 us  [body(): occ_all = lax.all_gather(later_occ, orb, axis=0, tiled=False)]
    all_to_all x2 -> x1, starting transfers between devices: 36.5 us -> 14.7 us  [body(): first = lax.all_to_all(later, orb, 0, 0, tiled=True)]
    dot_general x3 -> x0, matrix products: 16.8 us -> none  [the longest x1 9.12 us: body(): jnp.einsum('pmn,tnb->tpmb', lax.all_gather(masked, 'orb', axis=1, tiled=T...]
    all_to_all x2 -> x1, waiting for transfers between devices: 10.1 us -> 0.01 us  [body(): first = lax.all_to_all(later, orb, 0, 0, tiled=True)]
  transfers between devices with their start and end apart: 5 -> 2, of which waited for: 4 -> 0; matrix products, arithmetic and copies ran while one was open for 4% -> 0% of each run, Pallas kernels for 0% -> 1%
where the time goes in v2:
time: 147 us; the launch traced here: 146 us
  blocking collectives  111 us (76%)
  starting transfers between devices  14.7 us (10%)
  between operations  13.4 us (9%)
  Pallas kernels  5.26 us (4%)
  local copies, waits for them, and re-layouts  2.29 us (2%)
    all_gather x1, blocking collectives, body(): occ_all = lax.all_gather(later_occ, orb, axis=0, tiled=False)  44.3 us
    all_to_all x1, blocking collectives, body(): paired = lax.all_to_all(paired, share, 0, 0, tiled=True)  20.9 us
    all_to_all x1, blocking collectives, body(): everyone = lax.all_to_all(spread, orb, 0, 0, tiled=True)  15.7 us
    all_to_all x1, blocking collectives, body(): lax.all_to_all(by_row, ('x', 'y'), 0, 0, tiled=True)  15 us
    all_to_all x1, starting transfers between devices, body(): first = lax.all_to_all(later, orb, 0, 0, tiled=True)  14.7 us
    all_to_all x1, blocking collectives, body(): summed = lax.all_to_all(partial, share, 0, 0, tiled=True)  14.7 us
  transfers between devices with their start and end apart: 2, of which 0 were waited for; matrix products, arithmetic and copies ran while one was open for 0% of the time, Pallas kernels for 1%

profile of v2, /device:TPU:1, one launch (start us, length us, event | category | flops | bytes accessed | tf_op | source)
XLA Modules:
  0.0 146.4 jit_solution(10920408133225083573)
XLA Ops:
  6.5 0.0 copy-start.2
  6.5 0.0 copy-start.1
  6.5 0.0 all-gather.3.cloned.1.call-start
  6.5 1.8 %shard_map.46 = f32[16,16,256]{2,1,0:T(8,128)} custom-call(s32[4,4]{1,0:T(4,128)} %blocks_ref.3, f32[16,16,256]{2,1,0:T(8,128)} %slab_ref.1), custom_call_target="tpu_custom_call" | custom-call | tf_op jit(solution)/shard_map/pallas_call | solution.py:93
  8.4 15.0 %all_to_all.25 = f32[16,16,256]{2,1,0:T(8,128)} all-to-all(f32[16,16,256]{2,1,0:T(8,128)} %shard_map.46), channel_id=1, replica_groups=mesh['g'=4,'b'=2,'c'=2,'x'=4,'y'=4,'zh'=2] {'x','y'}, dimensions={0} | all-to-all | bytes 524288 | tf_op jit(solution)/shard_map/all_to_all | solution.py:100
  23.4 0.0 all-gather.3.cloned.1.call-update
  23.4 14.7 %all-to-all-start.1 = ((f32[16,16,256]{2,1,0:T(8,128)}), f32[16,16,256]{2,1,0:T(8,128)S(1)}, u32[]{:S(2)}, u32[]{:S(2)}) async-start(f32[16,16,256]{2,1,0:T(8,128)} %slab_ref.1), calls=%async_computation.1 | async-start | bytes 524288 | tf_op jit(solution)/shard_map/all_to_all | solution.py:104
  38.1 44.3 %all-gather = f32[32,16,256]{2,1,0:T(8,128)S(1)} all-gather(f32[2,16,256]{2,1,0:T(8,128)} %param.6), channel_id=2, replica_groups=mesh['g'=4,'b'=2,'c'=2,'x'=4,'y'=4,'zh'=2] {'g','b','c'}, dimensions={0}, use_global_device_ids=true | all-gather | bytes 557056 | tf_op jit(solution)/shard_map/all_gather | solution.py:105
  82.4 0.0 all-to-all-done.1.slab_ref
  82.4 0.0 copy-done.2
  82.4 0.0 copy-done.1
  82.5 1.5 %shard_map.47 = f32[64,8,256]{2,1,0:T(8,128)S(1)} custom-call(s32[4,4]{1,0:T(4,128)S(1)} %copy-done.2, f32[16,16,256]{2,1,0:T(8,128)S(1)} %all-to-all-done.1.slab_ref, f32[16,2,16,256]{3,2,1,0:T(8,128)S(1)} %bitcast.5, f32[2,256,256]{2,1,0:T(8,128)S(1)} %copy-done.1), custom_call_target="tpu_custom_call" | custom-call | tf_op jit(solution)/shard_map/pallas_call | solution.py:106
  83.9 20.9 %all_to_all.26.paired_ref = f32[64,8,256]{2,1,0:T(8,128)S(1)} all-to-all(f32[64,8,256]{2,1,0:T(8,128)S(1)} %shard_map.47), channel_id=1, replica_groups=mesh['g'=4,'b'=2,'c'=2,'x'=4,'y'=4,'zh'=2] {'b','c','x','y'}, dimensions={0} | all-to-all | bytes 1048576 | tf_op jit(solution)/shard_map/all_to_all | solution.py:113
  104.8 0.0 all-gather.3.cloned.1.call-done
  104.8 0.0 copy-start
  104.8 1.6 %copy-done = f32[2048,256]{1,0:T(8,128)S(1)} copy-done((f32[2048,256]{1,0:T(8,128)S(1)}, f32[2048,256]{1,0:T(8,128)}, u32[]{:S(2)}) %copy-start) | copy-done | bytes 2097176
  106.4 2.0 %shard_map.48 = f32[64,8,128]{2,1,0:T(8,128)S(1)} custom-call(f32[64,8,256]{2,1,0:T(8,128)S(1)} %all_to_all.26.paired_ref, f32[2,4,256,256]{3,2,1,0:T(8,128)S(1)} %bitcast.4), custom_call_target="tpu_custom_call" | custom-call | tf_op jit(solution)/shard_map/pallas_call | solution.py:117
  108.4 14.7 %all_to_all.27 = f32[64,8,128]{2,1,0:T(8,128)S(1)} all-to-all(f32[64,8,128]{2,1,0:T(8,128)S(1)} %shard_map.48), channel_id=1, replica_groups=mesh['g'=4,'b'=2,'c'=2,'x'=4,'y'=4,'zh'=2] {'b','c','x','y'}, dimensions={0} | all-to-all | bytes 524288 | tf_op jit(solution)/shard_map/all_to_all | solution.py:129
  123.1 0.1 reduce_sum.9
  123.1 15.7 %all_to_all.28 = f32[16,8,128]{2,1,0:T(8,128)S(1)} all-to-all(f32[16,8,128]{2,1,0:T(8,128)S(1)} %broadcast_in_dim.2), channel_id=1, replica_groups=mesh['g'=4,'b'=2,'c'=2,'x'=4,'y'=4,'zh'=2] {'g','b','c'}, dimensions={0} | all-to-all | bytes 131072 | tf_op jit(solution)/shard_map/all_to_all | solution.py:132
  138.9 0.6 copy.6
  (2 shorter events, 0.0 us)
Async XLA Ops:
  6.5 75.9 %copy-start.2 = (s32[4,4]{1,0:T(4,128)S(1)}, s32[4,4]{1,0:T(4,128)}, u32[]{:S(2)}) copy-start(s32[4,4]{1,0:T(4,128)} %blocks_ref.3) | copy-start | bytes 196
  6.5 75.9 %copy-start.1 = (f32[2,256,256]{2,1,0:T(8,128)S(1)}, f32[2,256,256]{2,1,0:T(8,128)}, u32[]{:S(2)}) copy-start(f32[2,256,256]{2,1,0:T(8,128)} %vir_ref.1) | copy-start | bytes 1572868
  6.5 98.3 %all-gather.3.cloned.1.call-start = ((), (), s32[]{:S(2)}) async-start(), calls=%async_computation.5 | async-start | bytes 2359296 | tf_op jit(solution)/shard_map/all_gather | solution.py:101
  23.4 59.0 %all-to-all-start.1 = ((f32[16,16,256]{2,1,0:T(8,128)}), f32[16,16,256]{2,1,0:T(8,128)S(1)}, u32[]{:S(2)}, u32[]{:S(2)}) async-start(f32[16,16,256]{2,1,0:T(8,128)} %slab_ref.1), calls=%async_computation.1 | async-start | bytes 524288 | tf_op jit(solution)/shard_map/all_to_all | solution.py:104
  104.8 1.6 %copy-start = (f32[2048,256]{1,0:T(8,128)S(1)}, f32[2048,256]{1,0:T(8,128)}, u32[]{:S(2)}) copy-start(f32[2048,256]{1,0:T(8,128)} %all-gather.3.cloned.1.call-done) | copy-start | bytes 6291460
Sparse Core Ops, SparseCore 0:
  23.5 79.8 all-gather.2

commit v3 on v2

--- a/solution.py
+++ b/solution.py
@@ -59,28 +59,27 @@
             out_ref[:, t * bands + g, :] = paired[g * dests:(g + 1) * dests]
 
 
-def respond(paired_ref, slab_ref, out_ref, total):
-    step = pl.program_id(0)
-    sources, planes = paired_ref.shape[0], 16
-    halves, _, count, norbit = slab_ref.shape
-    bands = pl.num_programs(0)
+def respond(paired_ref, slab_ref, out_ref, held, sems):
+    sources = paired_ref.shape[0]
+    bands, halves, count, norbit = held.shape
+    planes = 16
     run = count // planes
-
-    @pl.when(step == 0)
-    def _():
-        total[...] = jnp.zeros_like(total)
-
-    rows = [paired_ref[:, pl.ds(i * bands + step, 1), :].reshape(sources, norbit) for i in range(2)]
-    right = jnp.swapaxes(slab_ref[...].reshape(halves, planes, run, norbit), 0, 1).reshape(halves * count, norbit)
-    total[...] += dot3(split(jnp.concatenate(rows, axis=0)), split(right), NT_DIMS)
-
-    @pl.when(step == bands - 1)
-    def _():
-        whole = total[...].reshape(2, sources, halves * count)
-        chunks = whole.shape[-1] // LANES
-        for i in range(2):
-            for k in range(chunks):
-                out_ref[:, i * chunks + k, :] = whole[i, :, k * LANES:(k + 1) * LANES]
+    copies = [pltpu.make_async_copy(slab_ref.at[:, g], held.at[g], sems.at[g]) for g in range(bands)]
+    for copy in copies:
+        copy.start()
+    lefts = []
+    for g in range(bands):
+        lefts.append(split(jnp.concatenate([paired_ref[:, i * bands + g, :] for i in range(2)], axis=0)))
+    total = None
+    for g in range(bands):
+        copies[g].wait()
+        right = jnp.swapaxes(held[g].reshape(halves, planes, run, norbit), 0, 1).reshape(halves * count, norbit)
+        part = dot3(lefts[g], split(right), NT_DIMS)
+        total = part if total is None else total + part
+    chunks = halves * count // LANES
+    for i in range(2):
+        for k in range(chunks):
+            out_ref[:, i * chunks + k, :] = total[i * sources:(i + 1) * sources, k * LANES:(k + 1) * LANES]
 
 
 def body(slab, pair_blocks, occ_density, vir_density):
@@ -116,16 +115,15 @@
     per_row = times * total_aux // LANES
     partial = pl.pallas_call(
         respond,
-        grid=(bands,),
         out_shape=jax.ShapeDtypeStruct((dests, per_row, LANES), f32),
-        in_specs=[
-            pl.BlockSpec((dests, 2 * bands, norbit), lambda s: (0, 0, 0)),
-            pl.BlockSpec((halves, 1, planes * aux_here, norbit), lambda s: (0, s, 0, 0)),
+        in_specs=[VMEM, pl.BlockSpec(memory_space=pltpu.HBM)],
+        out_specs=VMEM,
+        scratch_shapes=[
+            pltpu.VMEM((bands, halves, planes * aux_here, norbit), f32),
+            pltpu.SemaphoreType.DMA((bands,)),
         ],
-        out_specs=pl.BlockSpec((dests, per_row, LANES), lambda s: (0, 0, 0)),
-        scratch_shapes=[pltpu.VMEM((2 * dests, total_aux), f32)],
-        compiler_params=PARAMS,
-    )(paired.reshape(dests, 2 * bands, norbit), gathered)
+        compiler_params=pltpu.CompilerParams(vmem_limit_bytes=53 << 20),
+    )(paired, gathered)
     summed = lax.all_to_all(partial, share, 0, 0, tiled=True)
     row = jnp.sum(summed, axis=0)
     spread = jnp.broadcast_to(row[None], (aux_here,) + row.shape)

time: 147 us -> 146 us (level)
  local copies, waits for them, and re-layouts: 2.29 us -> 0.69 us
    unnamed x6 -> x4, local copies, waits for them, and re-layouts: 1.6 us -> 0.01 us
where the time goes in v3:
time: 146 us; the launch traced here: 145 us
  blocking collectives  111 us (76%)
  starting transfers between devices  14.7 us (10%)
  between operations  13.4 us (9%)
  Pallas kernels  5.73 us (4%)
    all_gather x1, blocking collectives, body(): occ_all = lax.all_gather(later_occ, orb, axis=0, tiled=False)  44.3 us
    all_to_all x1, blocking collectives, body(): paired = lax.all_to_all(paired, share, 0, 0, tiled=True)  20.9 us
    all_to_all x1, blocking collectives, body(): everyone = lax.all_to_all(spread, orb, 0, 0, tiled=True)  15.7 us
    all_to_all x1, blocking collectives, body(): lax.all_to_all(by_row, ('x', 'y'), 0, 0, tiled=True)  15 us
    all_to_all x1, starting transfers between devices, body(): first = lax.all_to_all(later, orb, 0, 0, tiled=True)  14.7 us
    all_to_all x1, blocking collectives, body(): summed = lax.all_to_all(partial, share, 0, 0, tiled=True)  14.7 us
  transfers between devices with their start and end apart: 2, of which 0 were waited for; matrix products, arithmetic and copies ran while one was open for 0% of the time, Pallas kernels for 1%

profile of v3, /device:TPU:1, one launch (start us, length us, event | category | flops | bytes accessed | tf_op | source)
XLA Modules:
  0.0 145.3 jit_solution(16548036326055897945)
XLA Ops:
  6.5 0.0 copy-start.1
  6.5 0.0 copy-start
  6.5 0.0 all-gather.3.cloned.1.call-start
  6.5 1.8 %shard_map.46 = f32[16,16,256]{2,1,0:T(8,128)} custom-call(s32[4,4]{1,0:T(4,128)} %blocks_ref.3, f32[16,16,256]{2,1,0:T(8,128)} %slab_ref.1), custom_call_target="tpu_custom_call" | custom-call | tf_op jit(solution)/shard_map/pallas_call | solution.py:92
  8.4 15.0 %all_to_all.25 = f32[16,16,256]{2,1,0:T(8,128)} all-to-all(f32[16,16,256]{2,1,0:T(8,128)} %shard_map.46), channel_id=1, replica_groups=mesh['g'=4,'b'=2,'c'=2,'x'=4,'y'=4,'zh'=2] {'x','y'}, dimensions={0} | all-to-all | bytes 524288 | tf_op jit(solution)/shard_map/all_to_all | solution.py:99
  23.4 0.0 all-gather.3.cloned.1.call-update
  23.4 14.7 %all-to-all-start.1 = ((f32[16,16,256]{2,1,0:T(8,128)}), f32[16,16,256]{2,1,0:T(8,128)S(1)}, u32[]{:S(2)}, u32[]{:S(2)}) async-start(f32[16,16,256]{2,1,0:T(8,128)} %slab_ref.1), calls=%async_computation.1 | async-start | bytes 524288 | tf_op jit(solution)/shard_map/all_to_all | solution.py:103
  38.1 44.3 %all-gather = f32[32,16,256]{2,1,0:T(8,128)S(1)} all-gather(f32[2,16,256]{2,1,0:T(8,128)} %param.6), channel_id=2, replica_groups=mesh['g'=4,'b'=2,'c'=2,'x'=4,'y'=4,'zh'=2] {'g','b','c'}, dimensions={0}, use_global_device_ids=true | all-gather | bytes 557056 | tf_op jit(solution)/shard_map/all_gather | solution.py:104
  82.4 0.0 all-to-all-done.1.slab_ref
  82.4 0.0 copy-done.1
  82.4 0.0 copy-done
  82.4 1.5 %shard_map.47 = f32[64,8,256]{2,1,0:T(8,128)S(1)} custom-call(s32[4,4]{1,0:T(4,128)S(1)} %copy-done.1, f32[16,16,256]{2,1,0:T(8,128)S(1)} %all-to-all-done.1.slab_ref, f32[16,2,16,256]{3,2,1,0:T(8,128)S(1)} %bitcast.4, f32[2,256,256]{2,1,0:T(8,128)S(1)} %copy-done), custom_call_target="tpu_custom_call" | custom-call | tf_op jit(solution)/shard_map/pallas_call | solution.py:105
  83.9 20.9 %all_to_all.26.paired_ref = f32[64,8,256]{2,1,0:T(8,128)S(1)} all-to-all(f32[64,8,256]{2,1,0:T(8,128)S(1)} %shard_map.47), channel_id=1, replica_groups=mesh['g'=4,'b'=2,'c'=2,'x'=4,'y'=4,'zh'=2] {'b','c','x','y'}, dimensions={0} | all-to-all | bytes 1048576 | tf_op jit(solution)/shard_map/all_to_all | solution.py:112
  104.8 0.0 all-gather.3.cloned.1.call-done
  104.8 2.4 %shard_map.48 = f32[64,8,128]{2,1,0:T(8,128)S(1)} custom-call(f32[64,8,256]{2,1,0:T(8,128)S(1)} %all_to_all.26.paired_ref, f32[2,4,256,256]{3,2,1,0:T(8,128)} %bitcast.5), custom_call_target="tpu_custom_call" | custom-call | tf_op jit(solution)/shard_map/pallas_call | solution.py:116
  107.3 14.7 %all_to_all.27 = f32[64,8,128]{2,1,0:T(8,128)S(1)} all-to-all(f32[64,8,128]{2,1,0:T(8,128)S(1)} %shard_map.48), channel_id=1, replica_groups=mesh['g'=4,'b'=2,'c'=2,'x'=4,'y'=4,'zh'=2] {'b','c','x','y'}, dimensions={0} | all-to-all | bytes 524288 | tf_op jit(solution)/shard_map/all_to_all | solution.py:127
  121.9 0.1 reduce_sum.9
  122.0 15.7 %all_to_all.28 = f32[16,8,128]{2,1,0:T(8,128)S(1)} all-to-all(f32[16,8,128]{2,1,0:T(8,128)S(1)} %broadcast_in_dim.2), channel_id=1, replica_groups=mesh['g'=4,'b'=2,'c'=2,'x'=4,'y'=4,'zh'=2] {'g','b','c'}, dimensions={0} | all-to-all | bytes 131072 | tf_op jit(solution)/shard_map/all_to_all | solution.py:130
  137.8 0.6 copy.6
  (2 shorter events, 0.0 us)
Async XLA Ops:
  6.5 75.9 %copy-start.1 = (s32[4,4]{1,0:T(4,128)S(1)}, s32[4,4]{1,0:T(4,128)}, u32[]{:S(2)}) copy-start(s32[4,4]{1,0:T(4,128)} %blocks_ref.3) | copy-start | bytes 196
  6.5 75.9 %copy-start = (f32[2,256,256]{2,1,0:T(8,128)S(1)}, f32[2,256,256]{2,1,0:T(8,128)}, u32[]{:S(2)}) copy-start(f32[2,256,256]{2,1,0:T(8,128)} %vir_ref.1) | copy-start | bytes 1572868
  6.5 98.3 %all-gather.3.cloned.1.call-start = ((), (), s32[]{:S(2)}) async-start(), calls=%async_computation.5 | async-start | bytes 2359296 | tf_op jit(solution)/shard_map/all_gather | solution.py:100
  23.4 59.0 %all-to-all-start.1 = ((f32[16,16,256]{2,1,0:T(8,128)}), f32[16,16,256]{2,1,0:T(8,128)S(1)}, u32[]{:S(2)}, u32[]{:S(2)}) async-start(f32[16,16,256]{2,1,0:T(8,128)} %slab_ref.1), calls=%async_computation.1 | async-start | bytes 524288 | tf_op jit(solution)/shard_map/all_to_all | solution.py:103
Sparse Core Ops, SparseCore 0:
  23.5 79.8 all-gather.2

commit v4 on v3

--- a/solution.py
+++ b/solution.py
@@ -43,20 +43,24 @@
         rows_ref[m] = slab_ref[:, m, :] * mask
 
 
-def pairing(blocks_ref, slab_ref, occ_ref, vir_ref, out_ref):
-    peers, times, rows, norbit = occ_ref.shape
+def pairing(blocks_ref, slab_ref, occ_ref, vir_ref, out_ref, full):
+    groups, peers, rows, norbit = occ_ref.shape
+    times = vir_ref.shape[0]
+    each = rows // times
+    inner, bands = out_ref.shape[0], peers // out_ref.shape[0]
     count = blocks_ref.shape[0]
     mask = jnp.concatenate(
         [jnp.broadcast_to(block_row(blocks_ref, j, norbit), (norbit // count, norbit)) for j in range(count)], axis=0
     )
     slab = split(slab_ref[...].reshape(norbit, norbit) * mask)
-    dests = out_ref.shape[0]
-    bands = norbit // dests
     for t in range(times):
         mixed = split(dot3(slab, split(vir_ref[t]), NN_DIMS))
-        paired = dot3(split(occ_ref[:, t].reshape(norbit, norbit)), mixed, NN_DIMS)
-        for g in range(bands):
-            out_ref[:, t * bands + g, :] = paired[g * dests:(g + 1) * dests]
+        occ = [occ_ref[:, :, t * each + r, :].reshape(groups * peers, norbit) for r in range(each)]
+        full[t] = dot3(split(jnp.concatenate(occ, axis=0)), mixed, NN_DIMS).reshape(full.shape[1:])
+        for r in range(each):
+            for g in range(bands):
+                for n in range(inner):
+                    out_ref[n, :, r, t * bands + g, :] = full[t, r, :, g * inner + n, :]
 
 
 def respond(paired_ref, slab_ref, out_ref, held, sems):
@@ -87,7 +91,7 @@
     times = occ_density.shape[0]
     bands, pairs, cores, planes, halves = 4, 2, 2, 16, 2
     dests = pairs * cores * planes
-    orb, share, f32 = ("g", "b", "c"), ("b", "c", "x", "y"), jnp.float32
+    orb, share, f32 = ("g", "b", "c"), ("b", "c", "xa", "xb", "y"), jnp.float32
 
     by_row = pl.pallas_call(
         by_rows,
@@ -96,19 +100,23 @@
         out_specs=VMEM,
         compiler_params=WIDE,
     )(pair_blocks, slab)
-    own = lax.all_to_all(by_row, ("x", "y"), 0, 0, tiled=True).reshape(planes * aux_here, norbit)
+    own = lax.all_to_all(by_row, ("xa", "xb", "y"), 0, 0, tiled=True).reshape(planes * aux_here, norbit)
     gathered = lax.all_gather(own, ("zh", "g"), axis=0, tiled=True).reshape(halves, bands, planes * aux_here, norbit)
 
     later, later_occ, own = lax.optimization_barrier((slab, occ_density, own))
     first = lax.all_to_all(later, orb, 0, 0, tiled=True)
-    occ_all = lax.all_gather(later_occ, orb, axis=0, tiled=False)
+    groups, peers = 2, bands * pairs * cores
+    each = own_rows // groups
+    mine = lax.dynamic_slice_in_dim(later_occ, lax.axis_index("xb") * each, each, 1).reshape(times * each, norbit)
+    occ_all = lax.all_gather(lax.all_gather(mine, orb, axis=0, tiled=False), "xb", axis=0, tiled=False)
     paired = pl.pallas_call(
         pairing,
-        out_shape=jax.ShapeDtypeStruct((dests, 2 * bands, norbit), f32),
+        out_shape=jax.ShapeDtypeStruct((pairs * cores, groups, each, times * bands, norbit), f32),
         in_specs=[SMEM, VMEM, VMEM, VMEM],
         out_specs=VMEM,
+        scratch_shapes=[pltpu.VMEM((times, each, groups, peers, norbit), f32)],
         compiler_params=PARAMS,
-    )(pair_blocks, first, occ_all, vir_density)
+    )(pair_blocks, first, occ_all, vir_density).reshape(dests, times * bands, norbit)
     paired = lax.all_to_all(paired, share, 0, 0, tiled=True)
 
     total_aux = halves * planes * aux_here
@@ -132,8 +140,8 @@
 
 
 def solution(mesh):
-    fine = Mesh(mesh.devices.reshape(4, 2, 2, 4, 4, 2), ("g", "b", "c", "x", "y", "zh"))
-    orb, aux = ("g", "b", "c"), ("x", "y", "zh")
+    fine = Mesh(mesh.devices.reshape(4, 2, 2, 2, 2, 4, 2), ("g", "b", "c", "xa", "xb", "y", "zh"))
+    orb, aux = ("g", "b", "c"), ("xa", "xb", "y", "zh")
     in_specs = (P(aux, orb, None), P(), P(None, orb, None), P())
     out_specs = P(None, aux, None)
     return jax.shard_map(body, mesh=fine, in_specs=in_specs, out_specs=out_specs, check_vma=False)

time: 146 us -> 146 us (level)
    all_gather x1 -> x2, blocking collectives: 44.3 us -> 48.2 us  [the longest x1 39.7 us: body(): lax.all_gather(mine, orb, axis=0, tiled=False)]
    all_to_all x1, blocking collectives: 20.9 us -> 18 us  [body(): paired = lax.all_to_all(paired, share, 0, 0, tiled=True)]
where the time goes in v4:
time: 146 us; the launch traced here: 145 us
  blocking collectives  110 us (75%)
  starting transfers between devices  14.7 us (10%)
  between operations  13.4 us (9%)
  Pallas kernels  5.93 us (4%)
    all_gather x1, blocking collectives, body(): lax.all_gather(mine, orb, axis=0, tiled=False)  39.7 us
    all_to_all x1, blocking collectives, body(): paired = lax.all_to_all(paired, share, 0, 0, tiled=True)  18 us
    all_to_all x1, blocking collectives, body(): lax.all_to_all(by_row, ('xa', 'xb', 'y'), 0, 0, tiled=True)  15 us
    all_to_all x1, blocking collectives, body(): everyone = lax.all_to_all(spread, orb, 0, 0, tiled=True)  14.9 us
    all_to_all x1, starting transfers between devices, body(): first = lax.all_to_all(later, orb, 0, 0, tiled=True)  14.7 us
    all_to_all x1, blocking collectives, body(): summed = lax.all_to_all(partial, share, 0, 0, tiled=True)  14.2 us
    all_gather x1, blocking collectives, body(): lax.all_gather(lax.all_gather(mine, orb, axis=0, tiled=False), 'xb', axis...  8.53 us
  transfers between devices with their start and end apart: 2, of which 0 were waited for; matrix products, arithmetic and copies ran while one was open for 0% of the time, Pallas kernels for 1%

profile of v4, /device:TPU:1, one launch (start us, length us, event | category | flops | bytes accessed | tf_op | source)
XLA Modules:
  0.0 145.2 jit_solution(4413951851460707047)
XLA Ops:
  6.5 0.0 copy-start
  6.5 0.0 copy-start.2
  6.5 0.0 copy-start.1
  6.5 0.0 all-gather.3.cloned.1.call-start
  6.5 1.8 %shard_map.46 = f32[16,16,256]{2,1,0:T(8,128)} custom-call(s32[4,4]{1,0:T(4,128)} %blocks_ref.3, f32[16,16,256]{2,1,0:T(8,128)} %slab_ref.1), custom_call_target="tpu_custom_call" | custom-call | tf_op jit(solution)/shard_map/pallas_call | solution.py:96
  8.4 15.0 %all_to_all.25 = f32[16,16,256]{2,1,0:T(8,128)} all-to-all(f32[16,16,256]{2,1,0:T(8,128)} %shard_map.46), channel_id=1, replica_groups=mesh['g'=4,'b'=2,'c'=2,'xa'=2,'xb'=2,'y'=4,'zh'=2] {'xa','xb','y'}, dimensions={0} | all-to-all | bytes 524288 | tf_op jit(solution)/shard_map/all_to_all | solution.py:103
  23.4 0.0 all-gather.3.cloned.1.call-update
  23.4 14.7 %all-to-all-start.1 = ((f32[16,16,256]{2,1,0:T(8,128)}), f32[16,16,256]{2,1,0:T(8,128)S(1)}, u32[]{:S(2)}, u32[]{:S(2)}) async-start(f32[16,16,256]{2,1,0:T(8,128)} %slab_ref.1), calls=%async_computation.1 | async-start | bytes 524288 | tf_op jit(solution)/shard_map/all_to_all | solution.py:107
  38.1 0.0 copy-done
  38.1 39.7 %all_gather.12 = f32[16,16,256]{2,1,0:T(8,128)S(1)} all-gather(f32[1,16,256]{2,1,0:T(8,128)S(1)} %dynamic-slice_bitcast_fusion), channel_id=1, replica_groups=mesh['g'=4,'b'=2,'c'=2,'xa'=2,'xb'=2,'y'=4,'zh'=2] {'g','b','c'}, dimensions={0}, use_global_device_ids=true | all-gather | bytes 278528 | tf_op jit(solution)/shard_map/all_gather | solution.py:111
  77.8 8.5 %all-gather = f32[32,16,256]{2,1,0:T(8,128)S(1)} all-gather(f32[16,16,256]{2,1,0:T(8,128)S(1)} %all_gather.12), channel_id=2, replica_groups=mesh['g'=4,'b'=2,'c'=2,'xa'=2,'xb'=2,'y'=4,'zh'=2] {'xb'}, dimensions={0}, use_global_device_ids=true | all-gather | bytes 786432 | tf_op jit(solution)/shard_map/all_gather | solution.py:111
  86.3 0.0 all-to-all-done.1.slab_ref
  86.4 0.0 copy-done.2
  86.4 0.0 copy-done.1
  86.4 1.7 %shard_map.47 = f32[4,2,8,8,256]{4,3,2,1,0:T(8,128)S(1)} custom-call(s32[4,4]{1,0:T(4,128)S(1)} %copy-done.2, f32[16,16,256]{2,1,0:T(8,128)S(1)} %all-to-all-done.1.slab_ref, f32[2,16,16,256]{3,2,1,0:T(8,128)S(1)} %bitcast.7, f32[2,256,256]{2,1,0:T(8,128)S(1)} %copy-done.1), custom_call_target="tpu_custom_call" | custom-call | tf_op jit(solution)/shard_map/pallas_call | solution.py:112
  88.0 18.0 %all_to_all.26.paired_ref = f32[64,8,256]{2,1,0:T(8,128)S(1)} all-to-all(f32[64,8,256]{2,1,0:T(8,128)S(1)} %bitcast.8), channel_id=1, replica_groups=mesh['g'=4,'b'=2,'c'=2,'xa'=2,'xb'=2,'y'=4,'zh'=2] {'b','c','xa','xb','y'}, dimensions={0} | all-to-all | bytes 1048576 | tf_op jit(solution)/shard_map/all_to_all | solution.py:120
  106.0 0.0 all-gather.3.cloned.1.call-done
  106.0 2.4 %shard_map.48 = f32[64,8,128]{2,1,0:T(8,128)S(1)} custom-call(f32[64,8,256]{2,1,0:T(8,128)S(1)} %all_to_all.26.paired_ref, f32[2,4,256,256]{3,2,1,0:T(8,128)} %bitcast.9), custom_call_target="tpu_custom_call" | custom-call | tf_op jit(solution)/shard_map/pallas_call | solution.py:124
  108.5 14.2 %all_to_all.27 = f32[64,8,128]{2,1,0:T(8,128)S(1)} all-to-all(f32[64,8,128]{2,1,0:T(8,128)S(1)} %shard_map.48), channel_id=1, replica_groups=mesh['g'=4,'b'=2,'c'=2,'xa'=2,'xb'=2,'y'=4,'zh'=2] {'b','c','xa','xb','y'}, dimensions={0} | all-to-all | bytes 524288 | tf_op jit(solution)/shard_map/all_to_all | solution.py:135
  122.7 0.1 reduce_sum.9
  122.7 14.9 %all_to_all.28 = f32[16,8,128]{2,1,0:T(8,128)S(1)} all-to-all(f32[16,8,128]{2,1,0:T(8,128)S(1)} %broadcast_in_dim.2), channel_id=1, replica_groups=mesh['g'=4,'b'=2,'c'=2,'xa'=2,'xb'=2,'y'=4,'zh'=2] {'g','b','c'}, dimensions={0} | all-to-all | bytes 131072 | tf_op jit(solution)/shard_map/all_to_all | solution.py:138
  137.7 0.6 copy.6
  (3 shorter events, 0.1 us)
Async XLA Ops:
  6.5 31.6 %copy-start = (f32[2,16,256]{2,1,0:T(8,128)S(1)}, f32[2,16,256]{2,1,0:T(8,128)}, u32[]{:S(2)}) copy-start(f32[2,16,256]{2,1,0:T(8,128)} %param.6) | copy-start | bytes 98308
  6.5 79.8 %copy-start.2 = (s32[4,4]{1,0:T(4,128)S(1)}, s32[4,4]{1,0:T(4,128)}, u32[]{:S(2)}) copy-start(s32[4,4]{1,0:T(4,128)} %blocks_ref.3) | copy-start | bytes 196
  6.5 79.8 %copy-start.1 = (f32[2,256,256]{2,1,0:T(8,128)S(1)}, f32[2,256,256]{2,1,0:T(8,128)}, u32[]{:S(2)}) copy-start(f32[2,256,256]{2,1,0:T(8,128)} %vir_ref.1) | copy-start | bytes 1572868
  6.5 99.5 %all-gather.3.cloned.1.call-start = ((), (), s32[]{:S(2)}) async-start(), calls=%async_computation.5 | async-start | bytes 2359296 | tf_op jit(solution)/shard_map/all_gather | solution.py:104
  23.4 63.0 %all-to-all-start.1 = ((f32[16,16,256]{2,1,0:T(8,128)}), f32[16,16,256]{2,1,0:T(8,128)S(1)}, u32[]{:S(2)}, u32[]{:S(2)}) async-start(f32[16,16,256]{2,1,0:T(8,128)} %slab_ref.1), calls=%async_computation.1 | async-start | bytes 524288 | tf_op jit(solution)/shard_map/all_to_all | solution.py:107
Sparse Core Ops, SparseCore 0:
  23.5 73.7 all-gather.2
